TPU v7x, 32 devices: a whole 2x2x4 slice. The times are simulated.
32 devices in a mesh: groups: 2 (over y), ctx: 4 (over x, core), head: 4 (over z).
Axes of the slice: x: 2, y: 2, z: 4, core: 2. Of those that a mesh axis runs over, the one named last changes fastest.
Arguments:
- attn_out: bfloat16 [1024, 8192], P(('groups', 'ctx'), 'head'), parts along dimension 0, may hold values from -6 to 6
- out_weight: bfloat16 [8192, 7168], P('head', 'ctx'), may hold values from -0.0625 to 0.0625
- residual: bfloat16 [1024, 7168], P(('groups', 'ctx', 'head')), parts along dimension 0, may hold values from -6 to 6
- norm_gain: float32 [7168], replicated, may hold values from 0.1 to 1.9
- expert_ids: int32 [1024, 2], P(('groups', 'ctx', 'head')), parts along dimension 0, may hold values from 0 to 3, all different within a row; in each aligned block of 32 rows (0 to 31, 32 to 63, ...) at most 24 rows name the same one
- gate_codes: int32 [1024, 2], P(('groups', 'ctx', 'head')), parts along dimension 0, may hold values from 1 to 1024
- w_gate: bfloat16 [4, 7168, 2048], P('ctx', None, 'head'), may hold values from -0.0625 to 0.0625
- w_up: bfloat16 [4, 7168, 2048], P('ctx', None, 'head'), may hold values from -0.0625 to 0.0625
- w_down: bfloat16 [4, 2048, 7168], P('ctx', 'head'), may hold values from -0.125 to 0.125
Outputs:
- mixed: bfloat16 [1024, 7168], P(('groups', 'ctx', 'head')), parts along dimension 0
There are 2 independent parts, one for each index of `groups`. A program takes and returns all parts, laid end to end along the dimension named above; an argument that names none is the same for every part. Nothing has to cross between parts.
Inputs may be any that keep to these rules, and one draw needn't show every extreme that they name: `expert_ids`: each row names 2 different experts. In each aligned block of 32 rows no expert is named by more than 24 rows, a bound that some block reaches.
All inputs are finite; a program needn't handle non-finite values.
Results may differ from a plain program's by a relative error of at most 0.017.
Values may be sent and summed in bfloat16 or wider, within the bound.
A program may use at most 128 MiB of HBM per device.

v0:
```python
import jax
import jax.numpy as jnp
from jax import lax
from jax.sharding import PartitionSpec as P


def route_places(expert_ids, experts, capacity):
    flattened = expert_ids.reshape(-1)
    onehot = (flattened[:, None] == jnp.arange(experts, dtype=jnp.int32)[None, :]).astype(jnp.int32)
    before = jnp.cumsum(onehot, axis=0) - onehot
    slot_index = jnp.sum(onehot * before, axis=1)
    return (flattened * capacity + slot_index).reshape(expert_ids.shape)


def expert_apply(token_rows, w_gate, w_up, w_down):
    row_shape = token_rows.shape
    flattened = token_rows.reshape(-1, row_shape[-1])
    gate_proj = jnp.dot(flattened, w_gate[0], preferred_element_type=jnp.float32)
    up_proj = jnp.dot(flattened, w_up[0], preferred_element_type=jnp.float32)
    activation = (jax.nn.silu(gate_proj) * up_proj).astype(jnp.bfloat16)
    result = jnp.dot(activation, w_down[0], preferred_element_type=jnp.float32)
    return result.reshape(row_shape)


def local(attn_out, out_weight, residual, norm_gain, expert_ids, gate_codes, w_gate, w_up, w_down):
    ctx_count = lax.axis_size("ctx")
    rows_dev = residual.shape[0]
    model_width = residual.shape[1]
    partial_sums = jnp.dot(
        attn_out,
        lax.all_gather(out_weight, "ctx", axis=1, tiled=True),
        preferred_element_type=jnp.float32,
    )
    projected = lax.psum_scatter(
        partial_sums.astype(jnp.bfloat16), "head", scatter_dimension=0, tiled=True
    ).astype(jnp.float32)
    hidden_state = residual.astype(jnp.float32) + projected
    mean_square = jnp.mean(hidden_state * hidden_state, axis=1, keepdims=True)
    normed = (hidden_state * lax.rsqrt(mean_square + 1e-06) * norm_gain).astype(jnp.bfloat16)
    routes = expert_ids.shape[1]
    capacity = min(rows_dev, max(2, (3 * rows_dev * routes + 2 * ctx_count - 1) // (2 * ctx_count)))
    places = route_places(expert_ids, ctx_count, capacity)
    slot_range = jnp.arange(ctx_count * capacity, dtype=jnp.int32)
    select = jnp.any(slot_range[:, None, None] == places[None, :, :], axis=2).astype(jnp.bfloat16)
    outbound = jnp.dot(select, normed, preferred_element_type=jnp.float32).astype(jnp.bfloat16)
    outbound = outbound.reshape(ctx_count, capacity, model_width)
    arrived = lax.all_to_all(outbound, "ctx", split_axis=0, concat_axis=0, tiled=True)
    partial_out = expert_apply(
        lax.all_gather(arrived[:, None], "head", axis=1, tiled=True), w_gate, w_up, w_down
    )
    summed_out = lax.psum_scatter(
        partial_out.astype(jnp.bfloat16), "head", scatter_dimension=1, tiled=True
    ).astype(jnp.float32)
    returned = lax.all_to_all(
        summed_out.reshape(ctx_count, capacity, model_width).astype(jnp.bfloat16),
        "ctx",
        split_axis=0,
        concat_axis=0,
        tiled=True,
    ).astype(jnp.float32)
    gate_values = gate_codes.astype(jnp.float32)
    route_weights = 2.5 * gate_values / jnp.sum(gate_values, axis=1, keepdims=True)
    matching = places[:, :, None] == slot_range[None, None, :]
    mixing = jnp.sum(jnp.where(matching, route_weights[:, :, None], 0.0), axis=1)
    combined = jnp.dot(
        mixing,
        returned.reshape(ctx_count * capacity, model_width),
        precision=lax.Precision.HIGHEST,
        preferred_element_type=jnp.float32,
    )
    return (hidden_state + combined).astype(jnp.bfloat16)


def solution(mesh):
    in_specs = (
        P(("groups", "ctx"), "head"),
        P("head", "ctx"),
        P(("groups", "ctx", "head"), None),
        P(),
        P(("groups", "ctx", "head"), None),
        P(("groups", "ctx", "head"), None),
        P("ctx", None, "head"),
        P("ctx", None, "head"),
        P("ctx", "head", None),
    )
    out_specs = P(("groups", "ctx", "head"), None)
    return jax.shard_map(local, mesh=mesh, in_specs=in_specs, out_specs=out_specs, check_vma=False)
```

profile of v0, /device:TPU:27, one launch (start us, length us, event | category | flops | bytes accessed | tf_op | source)
XLA Modules:
  0.0 611.4 jit_solution(65080010222843663)
XLA Ops:
  6.5 0.0 copy-start
  6.5 0.0 all-gather.4.cloned.1.call-start
  6.5 0.7 all-gather.4.cloned.1.call-update
  7.3 0.0 copy-start.5
  7.3 0.0 copy-start.2
  7.3 0.0 copy-start.4
  7.3 0.0 reduce-scatter.3.cloned.1.call-start
  7.3 180.1 %all-gather.4.cloned.1.call-done = bf16[2048,7168]{1,0:T(8,128)(2,1)} async-done(((bf16[2048,1792]{1,0:T(8,128)(2,1)}), bf16[2048,7168]{1,0:T(8,128)(2,1)}) %all-gather.4.cloned.1.call-update) | async-done | bytes 29360144 | tf_op jit(solution)/shard_map/all_gather | solution.py:31
  187.4 0.0 copy-done
  187.4 14.6 %convolution_convert_fusion.1 = bf16[128,7168]{1,0:T(8,128)(2,1)} fusion(bf16[128,2048]{1,0:T(8,128)(2,1)S(1)} %copy-done, bf16[2048,7168]{1,0:T(8,128)(2,1)} %all-gather.4.cloned.1.call-done), kind=kOutput, calls=%fused_computation.1 | convolution fusion | flops 3759013888 | bytes 31719424 | tf_op jit(solution)/shard_map/dot_general | solution.py:29
  202.0 0.0 reduce-scatter.3.cloned.1.call-update
  202.1 0.0 all-gather.6.cloned.1.call-start
  202.1 0.0 copy-done.5
  202.1 0.1 copy.27
  202.2 0.1 eq.20
  202.3 0.1 fusion.14
  202.4 0.1 reduce_window_sum.11
  202.5 0.2 select_reduce_fusion.1
  202.7 0.1 reduce_sum.39
  202.8 0.1 copy.28
  202.9 0.1 fusion.15
  203.0 37.3 %reduce-scatter.3.cloned.1.call-done = bf16[32,7168]{1,0:T(8,128)(2,1)} async-done(((bf16[128,7168]{1,0:T(8,128)(2,1)}), bf16[32,7168]{1,0:T(8,128)(2,1)}) %reduce-scatter.3.cloned.1.call-update) | async-done | bytes 458768 | tf_op jit(solution)/shard_map/reduce_scatter | solution.py:34
  240.3 0.0 copy-done.2
  240.3 1.3 multiply_reduce_fusion
  241.6 0.0 copy-done.4
  241.6 1.6 convolution_convert_fusion.2
  243.2 20.1 %all_to_all.10 = bf16[4,24,7168]{2,1,0:T(8,128)(2,1)} all-to-all(bf16[4,24,7168]{2,1,0:T(8,128)(2,1)S(1)} %bitcast.35), channel_id=1, replica_groups=mesh['groups'=2,'ctx'=4,'head'=4] {'ctx'}, dimensions={0} | all-to-all | bytes 2752512 | tf_op jit(solution)/shard_map/all_to_all | solution.py:47
  263.3 0.0 all-gather.6.cloned.1.call-update
  263.3 0.0 all-reduce.3.cloned.1.call-start
  263.4 101.2 %all-gather.6.cloned.1.call-done = bf16[4,96,7168]{2,1,0:T(8,128)(2,1)} async-done(((bf16[4,24,7168]{2,1,0:T(8,128)(2,1)}), bf16[4,96,7168]{2,1,0:T(8,128)(2,1)}) %all-gather.6.cloned.1.call-update) | async-done | bytes 5505040 | tf_op jit(solution)/shard_map/all_gather | solution.py:49
  364.5 7.7 %fusion.4 = f32[384,512]{1,0:T(8,128)S(1)} fusion(bf16[384,7168]{1,0:T(8,128)(2,1)} %bitcast.38, bf16[1,7168,512]{2,1,0:T(8,128)(2,1)} %param.15), kind=kOutput, calls=%fused_computation.8 | convolution fusion | flops 2818572288 | bytes 13631488 | tf_op jit(solution)/shard_map/dot_general | solution.py:18
  372.3 0.0 copy-done.7
  372.3 0.0 slice-start.1
  372.3 6.4 %fusion.9 = bf16[384,512]{1,0:T(8,128)(2,1)S(1)} fusion(bf16[384,7168]{1,0:T(8,128)(2,1)S(1)} %bitcast.39, bf16[1,7168,512]{2,1,0:T(8,128)(2,1)} %param.16, f32[384,512]{1,0:T(8,128)S(1)} %fusion.4), kind=kOutput, calls=%fused_computation.12 | convolution fusion | flops 2819751936 | bytes 14024704 | tf_op jit(solution)/shard_map/dot_general | solution.py:19
  378.7 0.0 slice-done
  378.7 0.0 slice-done.1
  378.7 4.9 convolution_convert_fusion
  383.7 0.0 all-reduce.3.cloned.1.call-update
  383.7 0.0 copy-start.1
  383.7 0.6 copy-done.8
  384.3 0.6 dynamic-slice
  384.9 195.3 %all-reduce.3.cloned.1.call-done = bf16[4,4,24,7168]{3,2,1,0:T(8,128)(2,1)} async-done(((bf16[4,4,24,7168]{3,2,1,0:T(8,128)(2,1)}), bf16[4,4,24,7168]{3,2,1,0:T(8,128)(2,1)}) %all-reduce.3.cloned.1.call-update) | async-done | bytes 5505040
  580.2 3.2 dynamic-slice_bitcast_fusion
  583.4 3.9 all-to-all-start.1
  587.4 0.1 select_reduce_fusion
  587.5 15.9 %all-to-all-done.1 = bf16[4,24,7168]{2,1,0:T(8,128)(2,1)S(1)} async-done(((bf16[4,24,7168]{2,1,0:T(8,128)(2,1)}), bf16[4,24,7168]{2,1,0:T(8,128)(2,1)S(1)}, u32[]{:S(2)}, u32[]{:S(2)}) %all-to-all-start.1) | async-done | bytes 1376288 | tf_op jit(solution)/shard_map/all_to_all | solution.py:54
  603.4 0.0 copy-done.3
  603.4 1.5 fusion
  (12 shorter events, 0.1 us)
Async XLA Ops:
  6.5 180.9 %copy-start = (bf16[128,2048]{1,0:T(8,128)(2,1)S(1)}, bf16[128,2048]{1,0:T(8,128)(2,1)}, u32[]{:S(2)}) copy-start(bf16[128,2048]{1,0:T(8,128)(2,1)} %param.9) | copy-start | bytes 1572868
  6.5 180.9 %all-gather.4.cloned.1.call-start = ((), (), s32[]{:S(2)}) async-start(), calls=%async_computation.3 | async-start | bytes 36700160 | tf_op jit(solution)/shard_map/all_gather | solution.py:31
  7.3 194.8 %copy-start.5 = (s32[32,2]{0,1:T(2,128)S(1)}, s32[32,2]{0,1:T(2,128)}, u32[]{:S(2)}) copy-start(s32[32,2]{0,1:T(2,128)} %param.13) | copy-start | bytes 772
  7.3 233.0 %copy-start.2 = (bf16[32,7168]{1,0:T(8,128)(2,1)S(1)}, bf16[32,7168]{1,0:T(8,128)(2,1)}, u32[]{:S(2)}) copy-start(bf16[32,7168]{1,0:T(8,128)(2,1)} %param.11) | copy-start | bytes 1376260
  7.3 234.3 %copy-start.4 = (f32[7168]{0:T(1024)S(1)}, f32[7168]{0:T(1024)}, u32[]{:S(2)}) copy-start(f32[7168]{0:T(1024)} %param.12) | copy-start | bytes 86020
  7.3 233.0 %reduce-scatter.3.cloned.1.call-start = ((), (), s32[]{:S(2)}) async-start(), calls=%async_computation.4 | async-start | bytes 2293760 | tf_op jit(solution)/shard_map/reduce_scatter | solution.py:34
  202.1 162.5 %all-gather.6.cloned.1.call-start = ((), (), s32[]{:S(2)}) async-start(), calls=%async_computation.5 | async-start | bytes 6881280 | tf_op jit(solution)/shard_map/all_gather | solution.py:49
  263.3 316.9 %all-reduce.3.cloned.1.call-start = ((), (), s32[]{:S(2)}) async-start(), calls=%async_computation.6 | async-start | bytes 11010048
  364.5 7.8 %copy-start.7 = (bf16[4,96,7168]{2,1,0:T(8,128)(2,1)S(1)}, bf16[4,96,7168]{2,1,0:T(8,128)(2,1)}, u32[]{:S(2)}) copy-start(bf16[4,96,7168]{2,1,0:T(8,128)(2,1)} %all-gather.6.cloned.1.call-done) | copy-start | bytes 16515076
  364.5 14.2 %slice-start = ((s8[7340032]{0:T(1024)(128)(4,1)}), s8[4194304]{0:T(1024)(128)(4,1)S(1)}, s32[]{:S(2)}) async-start(s8[7340032]{0:T(1024)(128)(4,1)} %bitcast.36), calls=%async_computation.7 | async-start | bytes 8388608
  372.3 6.4 %slice-start.1 = ((s8[7340032]{0:T(1024)(128)(4,1)}), s8[3145728]{0:T(1024)(128)(4,1)S(1)}, s32[]{:S(2)}) async-start(s8[7340032]{0:T(1024)(128)(4,1)} %bitcast.36), calls=%async_computation.8 | async-start | bytes 6291456
  383.6 0.7 copy-start.8
  383.7 203.7 %copy-start.6 = (s32[32,2]{0,1:T(2,128)S(1)}, s32[32,2]{0,1:T(2,128)}, u32[]{:S(2)}) copy-start(s32[32,2]{0,1:T(2,128)} %param.14) | copy-start | bytes 772
  383.7 219.8 %copy-start.3 = (bf16[32,7168]{1,0:T(8,128)(2,1)S(1)}, bf16[32,7168]{1,0:T(8,128)(2,1)}, u32[]{:S(2)}) copy-start(bf16[32,7168]{1,0:T(8,128)(2,1)} %reduce-scatter.3.cloned.1.call-done) | copy-start | bytes 1376260
  383.7 221.2 %copy-start.1 = (bf16[128,2048]{1,0:T(8,128)(2,1)S(1)}, bf16[128,2048]{1,0:T(8,128)(2,1)}, u32[]{:S(2)}) copy-start(bf16[128,2048]{1,0:T(8,128)(2,1)} %param.9) | copy-start | bytes 1572868
  583.4 20.0 %all-to-all-start.1 = ((bf16[4,24,7168]{2,1,0:T(8,128)(2,1)}), bf16[4,24,7168]{2,1,0:T(8,128)(2,1)S(1)}, u32[]{:S(2)}, u32[]{:S(2)}) async-start(bf16[4,24,7168]{2,1,0:T(8,128)(2,1)} %dynamic-slice_bitcast_fusion), calls=%async_computation.2 | async-start | bytes 2752512 | tf_op jit(solution)/shard_map/all_to_all | solution.py:54
Sparse Core Ops, SparseCore 0:
  8.9 178.4 all-gather.3
  202.2 38.0 reduce-scatter.2
  263.4 101.0 all-gather.5
  383.8 196.3 all-reduce.2
where the time goes:
time: 617 us; the launch traced here: 611 us
  waiting for transfers between devices  531 us (86%)
  matrix products  36.7 us (6%)
  blocking collectives  20.1 us (3%)
  between operations  13.3 us (2%)
    unnamed x5, waiting for transfers between devices  196 us
    all_gather x1, waiting for transfers between devices, local(): lax.all_gather(out_weight, 'ctx', axis=1, tiled=True)  180 us
    all_gather x1, waiting for transfers between devices, local(): lax.all_gather(arrived[:, None], 'head', axis=1, tiled=True)  101 us
    reduce_scatter x1, waiting for transfers between devices, local(): lax.psum_scatter(partial_sums.astype(jnp.bfloat16), 'head', scatter_dimen...  37.3 us
    all_to_all x1, blocking collectives, local(): lax.all_to_all(outbound, 'ctx', split_axis=0, concat_axis=0, tiled=True)  20.1 us
    all_to_all x1, waiting for transfers between devices, local(): lax.all_to_all(summed_out.reshape(ctx_count, capacity, model_width).astyp...  15.9 us
    dot_general x1, matrix products, local(): jnp.dot(attn_out, lax.all_gather(out_weight, 'ctx', axis=1, tiled=True),...  14.6 us
  transfers between devices with their start and end apart: 5, of which 5 were waited for; matrix products, arithmetic and copies ran while one was open for 0% of the time, Pallas kernels for 0%

commit v1 on v0

--- a/solution.py
+++ b/solution.py
@@ -71,6 +71,36 @@
     return (hidden_state + combined).astype(jnp.bfloat16)
 
 
+def local_dense(attn_out, out_weight, residual, norm_gain, expert_ids, gate_codes, w_gate, w_up, w_down):
+    ctx_count, head_count = lax.axis_size("ctx"), lax.axis_size("head")
+    rows_dev, model_width = residual.shape
+    expert = lax.axis_index("ctx")
+    attn = lax.all_gather(attn_out, "ctx", axis=0, tiled=True)
+    partial = jnp.dot(attn, out_weight, preferred_element_type=jnp.float32).astype(jnp.bfloat16)
+    partial = partial.reshape(ctx_count, head_count, rows_dev, -1).transpose(1, 0, 2, 3)
+    partial = partial.reshape(head_count * ctx_count * rows_dev, -1)
+    summed = lax.psum_scatter(partial, "head", scatter_dimension=0, tiled=True)
+    summed = summed.reshape(ctx_count, rows_dev, -1)
+    projected = lax.all_to_all(summed, "ctx", split_axis=0, concat_axis=2, tiled=True)
+    hidden_state = residual.astype(jnp.float32) + projected.reshape(rows_dev, model_width).astype(jnp.float32)
+    mean_square = jnp.mean(hidden_state * hidden_state, axis=1, keepdims=True)
+    normed = (hidden_state * lax.rsqrt(mean_square + 1e-06) * norm_gain).astype(jnp.bfloat16)
+    gate_values = gate_codes.astype(jnp.float32)
+    route_weights = 2.5 * gate_values / jnp.sum(gate_values, axis=1, keepdims=True)
+    named = expert_ids[:, :, None] == jnp.arange(ctx_count, dtype=jnp.int32)
+    weights = jnp.sum(jnp.where(named, route_weights[:, :, None], 0.0), axis=1)
+    weights = lax.all_gather(weights, ("ctx", "head"), axis=0, tiled=True)
+    mine = jnp.sum(jnp.where(jnp.arange(ctx_count) == expert, weights, 0.0), axis=1, keepdims=True)
+    rows = lax.all_gather(normed, ("ctx", "head"), axis=0, tiled=True)
+    gate_proj = jnp.dot(rows, w_gate[0], preferred_element_type=jnp.float32)
+    up_proj = jnp.dot(rows, w_up[0], preferred_element_type=jnp.float32)
+    activation = (jax.nn.silu(gate_proj) * up_proj).astype(jnp.bfloat16)
+    out = jnp.dot(activation, w_down[0], preferred_element_type=jnp.float32)
+    out = jnp.where(mine == 0.0, 0.0, out * mine).astype(jnp.bfloat16)
+    combined = lax.psum_scatter(out, ("ctx", "head"), scatter_dimension=0, tiled=True)
+    return (hidden_state + combined.astype(jnp.float32)).astype(jnp.bfloat16)
+
+
 def solution(mesh):
     in_specs = (
         P(("groups", "ctx"), "head"),
@@ -84,4 +114,6 @@
         P("ctx", "head", None),
     )
     out_specs = P(("groups", "ctx", "head"), None)
-    return jax.shard_map(local, mesh=mesh, in_specs=in_specs, out_specs=out_specs, check_vma=False)
+    dense = 2 * mesh.shape["ctx"] <= 8
+    body = local_dense if dense else local
+    return jax.shard_map(body, mesh=mesh, in_specs=in_specs, out_specs=out_specs, check_vma=False)

time: 617 us -> 289 us (0.47)
  waiting for transfers between devices: 531 us -> 193 us
  blocking collectives: 20.1 us -> 39.5 us
    all_gather x2, waiting for transfers between devices: 281 us -> 63.3 us  [the longest x1 38.6 us: local_dense(): rows = lax.all_gather(normed, ('ctx', 'head'), axis=0, tiled=True)]
    unnamed x5 -> x4, waiting for transfers between devices: 196 us -> 0.76 us
    reduce_scatter x1 -> x2, waiting for transfers between devices: 37.3 us -> 129 us  [the longest x1 91.2 us: local_dense(): lax.psum_scatter(out, ('ctx', 'head'), scatter_dimension=0, tiled=True)]
    all_gather x0 -> x1, blocking collectives: none -> 29 us  [local_dense(): weights = lax.all_gather(weights, ('ctx', 'head'), axis=0, tiled=True)]
    all_to_all x1 -> x0, waiting for transfers between devices: 15.9 us -> none  [local(): lax.all_to_all(summed_out.reshape(ctx_count, capacity, model_width).astyp...]
    all_to_all x1, blocking collectives: 20.1 us -> 10.5 us  [local_dense(): lax.all_to_all(summed, 'ctx', split_axis=0, concat_axis=2, tiled=True)]
    dot_general x6 -> x4, matrix products: 36.7 us -> 33.4 us  [the longest x1 9.3 us: local_dense(): out = jnp.dot(activation, w_down[0], preferred_element_type=jnp.float32)]
  transfers between devices with their start and end apart: 5 -> 4, of which waited for: 5 -> 4; matrix products, arithmetic and copies ran while one was open for 0% -> 0% of each run, Pallas kernels for 0% -> 0%
where the time goes in v1:
time: 289 us; the launch traced here: 285 us
  waiting for transfers between devices  193 us (67%)
  blocking collectives  39.5 us (14%)
  matrix products  33.4 us (12%)
  between operations  13.3 us (5%)
  other arithmetic  3.3 us (1%)
    reduce_scatter x1, waiting for transfers between devices, local_dense(): lax.psum_scatter(out, ('ctx', 'head'), scatter_dimension=0, tiled=True)  91.2 us
    all_gather x1, waiting for transfers between devices, local_dense(): rows = lax.all_gather(normed, ('ctx', 'head'), axis=0, tiled=True)  38.6 us
    reduce_scatter x1, waiting for transfers between devices, local_dense(): summed = lax.psum_scatter(partial, 'head', scatter_dimension=0, tiled=True)  38.2 us
    all_gather x1, blocking collectives, local_dense(): weights = lax.all_gather(weights, ('ctx', 'head'), axis=0, tiled=True)  29 us
    all_gather x1, waiting for transfers between devices, local_dense(): attn = lax.all_gather(attn_out, 'ctx', axis=0, tiled=True)  24.7 us
    all_to_all x1, blocking collectives, local_dense(): lax.all_to_all(summed, 'ctx', split_axis=0, concat_axis=2, tiled=True)  10.5 us
    dot_general x1, matrix products, local_dense(): out = jnp.dot(activation, w_down[0], preferred_element_type=jnp.float32)  9.3 us
    dot_general x1, matrix products, local_dense(): gate_proj = jnp.dot(rows, w_gate[0], preferred_element_type=jnp.float32)  9.3 us
  transfers between devices with their start and end apart: 4, of which 4 were waited for; matrix products, arithmetic and copies ran while one was open for 0% of the time, Pallas kernels for 0%

profile of v1, /device:TPU:27, one launch (start us, length us, event | category | flops | bytes accessed | tf_op | source)
XLA Modules:
  0.0 285.4 jit_solution(12144318225751169962)
XLA Ops:
  6.5 0.0 all-gather.4.cloned.1.call-start
  6.5 0.7 all-gather.4.cloned.1.call-update
  7.3 0.0 reduce-scatter.3.cloned.1.call-start
  7.3 24.7 %all-gather.4.cloned.1.call-done = bf16[512,2048]{1,0:T(8,128)(2,1)} async-done(((bf16[128,2048]{1,0:T(8,128)(2,1)}), bf16[512,2048]{1,0:T(8,128)(2,1)}) %all-gather.4.cloned.1.call-update) | async-done | bytes 2097168 | tf_op jit(solution)/shard_map/all_gather | solution.py:78
  32.0 7.7 %convolution_convert_fusion = bf16[512,1792]{1,0:T(8,128)(2,1)S(1)} fusion(bf16[512,2048]{1,0:T(8,128)(2,1)} %all-gather.4.cloned.1.call-done, bf16[2048,1792]{1,0:T(8,128)(2,1)} %param.10), kind=kOutput, calls=%fused_computation.6 | convolution fusion | flops 3759013888 | bytes 11272192 | tf_op jit(solution)/shard_map/dot_general | solution.py:79
  39.7 0.0 copy-start
  39.7 0.0 copy-start.1
  39.7 0.0 copy-start.2
  39.7 0.0 copy-start.3
  39.7 1.4 copy.22
  41.1 0.0 reduce-scatter.3.cloned.1.call-update
  41.1 0.0 all-gather.6.cloned.1.call-start
  41.2 38.2 %reduce-scatter.3.cloned.1.call-done = bf16[128,1792]{1,0:T(8,128)(2,1)} async-done(((bf16[512,1792]{1,0:T(8,128)(2,1)}), bf16[128,1792]{1,0:T(8,128)(2,1)}) %reduce-scatter.3.cloned.1.call-update) | async-done | bytes 458768 | tf_op jit(solution)/shard_map/reduce_scatter | solution.py:82
  79.4 10.5 %all_to_all.4 = bf16[4,32,1792]{2,1,0:T(8,128)(2,1)S(1)} all-to-all(bf16[4,32,1792]{2,1,0:T(8,128)(2,1)} %bitcast.40), channel_id=1, replica_groups=mesh['groups'=2,'ctx'=4,'head'=4] {'ctx'}, dimensions={0} | all-to-all | bytes 917504 | tf_op jit(solution)/shard_map/all_to_all | solution.py:84
  89.9 0.1 convert_bitcast_fusion
  89.9 0.6 copy.23
  90.5 0.2 copy.25
  90.7 0.0 copy-done
  90.7 0.2 multiply_reduce_fusion
  91.0 0.0 copy-done.1
  91.0 0.9 multiply_convert_fusion
  91.9 0.0 all-gather.6.cloned.1.call-update
  91.9 0.0 reduce-scatter.5.cloned.1.call-start
  92.0 0.0 copy-done.2
  92.0 0.0 copy-done.3
  92.0 29.0 %all-gather = f32[16,32,4]{1,2,0:T(4,128)S(1)} all-gather(f32[1,32,4]{1,2,0:T(4,128)S(1)} %bitcast.41), channel_id=1, replica_groups=mesh['groups'=2,'ctx'=4,'head'=4] {'ctx','head'}, dimensions={0}, use_global_device_ids=true | all-gather | bytes 8704 | tf_op jit(solution)/shard_map/all_gather | solution.py:92
  121.1 0.1 reshape.38
  121.2 0.1 select_reduce_fusion
  121.3 38.6 %all-gather.6.cloned.1.call-done = bf16[512,7168]{1,0:T(8,128)(2,1)} async-done(((bf16[32,7168]{1,0:T(8,128)(2,1)}), bf16[512,7168]{1,0:T(8,128)(2,1)}) %all-gather.6.cloned.1.call-update) | async-done | bytes 7340048 | tf_op jit(solution)/shard_map/all_gather | solution.py:94
  159.9 0.0 copy-start.4
  159.9 9.3 %fusion.3 = f32[512,512]{1,0:T(8,128)S(1)} fusion(bf16[512,7168]{1,0:T(8,128)(2,1)} %all-gather.6.cloned.1.call-done, bf16[1,7168,512]{2,1,0:T(8,128)(2,1)} %param.15), kind=kOutput, calls=%fused_computation.4 | convolution fusion | flops 3758096384 | bytes 15728640 | tf_op jit(solution)/shard_map/dot_general | solution.py:95
  169.2 0.0 copy-done.4
  169.2 7.2 %fusion.8 = bf16[512,512]{1,0:T(8,128)(2,1)S(1)} fusion(bf16[512,7168]{1,0:T(8,128)(2,1)S(1)} %copy-done.4, bf16[1,7168,512]{2,1,0:T(8,128)(2,1)} %param.16, f32[512,512]{1,0:T(8,128)S(1)} %fusion.3), kind=kOutput, calls=%fused_computation.8 | convolution fusion | flops 3759669248 | bytes 16252928 | tf_op jit(solution)/shard_map/dot_general | solution.py:96
  176.4 9.3 %select_convert_fusion = bf16[512,7168]{1,0:T(8,128)(2,1)} fusion(bf16[512,512]{1,0:T(8,128)(2,1)S(1)} %fusion.8, bf16[1,512,7168]{2,1,0:T(8,128)(2,1)} %param.17, f32[512]{0:T(512)S(1)} %select_reduce_fusion, pred[512]{0:T(512)(128)(4,1)S(1)} %broadcast_compare_fusion), kind=kOutput, calls=%fused_computation | convolution fusion | flops 3769106432 | bytes 15206912 | tf_op jit(solution)/shard_map/dot_general | solution.py:98
  185.7 0.0 reduce-scatter.5.cloned.1.call-update
  185.7 91.2 %reduce-scatter.5.cloned.1.call-done = bf16[32,7168]{1,0:T(8,128)(2,1)} async-done(((bf16[512,7168]{1,0:T(8,128)(2,1)}), bf16[32,7168]{1,0:T(8,128)(2,1)}) %reduce-scatter.5.cloned.1.call-update) | async-done | bytes 458768 | tf_op jit(solution)/shard_map/reduce_scatter | solution.py:100
  276.9 1.9 add_convert_fusion
  (7 shorter events, 0.1 us)
Async XLA Ops:
  6.5 25.4 %all-gather.4.cloned.1.call-start = ((), (), s32[]{:S(2)}) async-start(), calls=%async_computation.3 | async-start | bytes 2621440 | tf_op jit(solution)/shard_map/all_gather | solution.py:78
  7.3 72.1 %reduce-scatter.3.cloned.1.call-start = ((), (), s32[]{:S(2)}) async-start(), calls=%async_computation.4 | async-start | bytes 2293760 | tf_op jit(solution)/shard_map/reduce_scatter | solution.py:82
  39.7 51.1 %copy-start = (bf16[32,7168]{1,0:T(8,128)(2,1)S(1)}, bf16[32,7168]{1,0:T(8,128)(2,1)}, u32[]{:S(2)}) copy-start(bf16[32,7168]{1,0:T(8,128)(2,1)} %param.11) | copy-start | bytes 1376260
  39.7 51.3 %copy-start.1 = (f32[7168]{0:T(1024)S(1)}, f32[7168]{0:T(1024)}, u32[]{:S(2)}) copy-start(f32[7168]{0:T(1024)} %param.12) | copy-start | bytes 86020
  39.7 52.3 %copy-start.2 = (s32[32,2]{0,1:T(2,128)S(1)}, s32[32,2]{0,1:T(2,128)}, u32[]{:S(2)}) copy-start(s32[32,2]{0,1:T(2,128)} %param.14) | copy-start | bytes 772
  39.7 52.3 %copy-start.3 = (s32[32,2]{0,1:T(2,128)S(1)}, s32[32,2]{0,1:T(2,128)}, u32[]{:S(2)}) copy-start(s32[32,2]{0,1:T(2,128)} %param.13) | copy-start | bytes 772
  41.1 118.8 %all-gather.6.cloned.1.call-start = ((), (), s32[]{:S(2)}) async-start(), calls=%async_computation.5 | async-start | bytes 7798784 | tf_op jit(solution)/shard_map/all_gather | solution.py:94
  91.9 185.0 %reduce-scatter.5.cloned.1.call-start = ((), (), s32[]{:S(2)}) async-start(), calls=%async_computation.6 | async-start | bytes 7798784 | tf_op jit(solution)/shard_map/reduce_scatter | solution.py:100
  159.9 9.3 %copy-start.4 = (bf16[512,7168]{1,0:T(8,128)(2,1)S(1)}, bf16[512,7168]{1,0:T(8,128)(2,1)}, u32[]{:S(2)}) copy-start(bf16[512,7168]{1,0:T(8,128)(2,1)} %all-gather.6.cloned.1.call-done) | copy-start | bytes 22020100
Sparse Core Ops, SparseCore 0:
  8.9 23.0 all-gather.3
  41.2 38.0 reduce-scatter.2
  92.0 67.7 all-gather.5
  185.8 91.0 reduce-scatter.4

commit v2 on v0

--- a/solution.py
+++ b/solution.py
@@ -1,6 +1,8 @@
 import jax
 import jax.numpy as jnp
 from jax import lax
+from jax.experimental import pallas as pl
+from jax.experimental.pallas import tpu as pltpu
 from jax.sharding import PartitionSpec as P
 
 
@@ -71,6 +73,348 @@
     return (hidden_state + combined).astype(jnp.bfloat16)
 
 
+BF16, F32 = jnp.bfloat16, jnp.float32
+SEMS = 72
+
+
+def layer_kernel(
+    attn, out_w, resid, gain, route_w, gate_w, up_w, down_w, out,
+    attn_all, work, gate_v, up_v, down_v, res_cols, part, arrived, hidden, scaled,
+    gate_acc, up_acc, square_sum, act, route_all, mine,
+    core_in, core_x_in, head_in, last_out, last_in, send, recv, local_sem,
+):
+    c, h = lax.axis_index("ctx"), lax.axis_index("head")
+    x, k = c // 2, c % 2
+    rows = resid.shape[0]
+    span, group = 4 * rows, 16 * rows
+    cols = part.shape[2]
+    tile = 256 if cols % 256 == 0 else 128
+    tiles = cols // tile
+    hidden_units = gate_acc.shape[1]
+
+    ctx_of = [c, 2 * x + (1 - k), 2 * (1 - x) + k, 2 * (1 - x) + (1 - k)]
+    to = [lax.rem(h + d, 4) for d in range(4)]
+    source = [lax.rem(h + 4 - d, 4) for d in range(4)]
+    SIB, ACROSS, DIAG = 1, 2, 3
+
+    def at(start, size):
+        return pl.ds(pl.multiple_of(start, size), size)
+
+    def cols_at(start):
+        return pl.ds(pl.multiple_of(start, 128), tile)
+
+    def remote(src, dst, number, j=0, d=0, back=False):
+        head = (source if back else to)[d]
+        return pltpu.make_async_remote_copy(
+            src_ref=src, dst_ref=dst, send_sem=send.at[number], recv_sem=recv.at[number],
+            device_id={"ctx": ctx_of[j], "head": head}, device_id_type=pl.DeviceIdType.MESH,
+        )
+
+    started = []
+
+    def push(src, dst, number, j=0, d=0):
+        copy = remote(src, dst, number, j, d)
+        copy.start()
+        started.append(copy)
+
+    def landed(dst, number, j=0, d=0):
+        remote(dst, dst, number, j, d, back=True).wait_recv()
+
+    barrier = pltpu.get_barrier_semaphore()
+    for j in range(4):
+        for d in range(4):
+            if (j, d) != (0, 0):
+                pl.semaphore_signal(
+                    barrier, inc=1, device_id={"ctx": ctx_of[j], "head": to[d]},
+                    device_id_type=pl.DeviceIdType.MESH,
+                )
+
+    depth = out_w.shape[0]
+    own_copies = [
+        pltpu.make_async_copy(attn, attn_all.at[c], local_sem.at[0]),
+        pltpu.make_async_copy(out_w, work.at[pl.ds(0, depth)], local_sem.at[1]),
+        pltpu.make_async_copy(resid.at[:, at(c * cols, cols)], res_cols.at[at(c * rows, rows)], local_sem.at[2]),
+        pltpu.make_async_copy(gate_w.at[0], gate_v, local_sem.at[3]),
+        pltpu.make_async_copy(up_w.at[0], up_v, local_sem.at[4]),
+        pltpu.make_async_copy(down_w.at[0], down_v, local_sem.at[5]),
+    ]
+    for copy in own_copies:
+        copy.start()
+    pl.semaphore_wait(barrier, 15)
+
+    push(attn, attn_all.at[c], 0, ACROSS)
+    push(attn, attn_all.at[c], 1, SIB)
+    for j in (1, 2, 3):
+        push(resid.at[:, at(ctx_of[j] * cols, cols)], res_cols.at[at(c * rows, rows)], 2 + j, j)
+    for j in range(4):
+        for d in range(4):
+            if (j, d) != (0, 0):
+                push(route_w, route_all.at[at(h * span + c * rows, rows)], 6 + 4 * j + d - 1, j, d)
+    route_all[at(h * span + c * rows, rows), :] = route_w[...]
+
+    def project(j):
+        block = ctx_of[j]
+
+        def step(t, _):
+            column = cols_at(t * tile)
+            y = jnp.dot(attn_all[block], work[pl.ds(0, depth), column], preferred_element_type=F32).astype(BF16)
+            for i in range(4):
+                part[i, at(block * rows, rows), column] = y[i * rows:(i + 1) * rows]
+            return 0
+
+        lax.fori_loop(0, tiles, step, 0)
+        for d in (2, 1, 3):
+            place = at(block * rows, rows)
+            push(part.at[to[d], place], arrived.at[d - 1, place], 21 + 3 * j + d - 1, 0, d)
+
+    own_copies[0].wait()
+    own_copies[1].wait()
+    project(0)
+    landed(attn_all.at[ctx_of[SIB]], 1, SIB)
+    project(1)
+    landed(attn_all.at[ctx_of[ACROSS]], 0, ACROSS)
+    push(attn_all.at[ctx_of[ACROSS]], attn_all.at[ctx_of[ACROSS]], 2, SIB)
+    project(2)
+    landed(attn_all.at[ctx_of[DIAG]], 2, SIB)
+    project(3)
+
+    own_copies[2].wait()
+    for j in (1, 2, 3):
+        landed(res_cols.at[at(ctx_of[j] * rows, rows)], 2 + j, j)
+    for j in range(4):
+        for d in (1, 2, 3):
+            landed(arrived.at[d - 1, at(ctx_of[j] * rows, rows)], 21 + 3 * j + d - 1, 0, d)
+
+    def add_up(t, _):
+        column = cols_at(t * tile)
+        total = part[h, :, column].astype(F32) + res_cols[:, column].astype(F32)
+        for d in range(3):
+            total = total + arrived[d, :, column].astype(F32)
+        hidden[c, at(h * span, span), column] = total.astype(BF16)
+        return 0
+
+    lax.fori_loop(0, tiles, add_up, 0)
+
+    def block_of(j, d):
+        return hidden.at[ctx_of[j], at(source[d] * span, span)]
+
+    for d in (2, 1, 3):
+        push(block_of(0, 0), block_of(0, 0), 33 + d - 1, 0, d)
+    push(block_of(0, 0), block_of(0, 0), 36, ACROSS)
+    push(block_of(0, 0), block_of(0, 0), 40, SIB)
+
+    square_sum[...] = jnp.zeros_like(square_sum)
+    gate_acc[...] = jnp.zeros_like(gate_acc)
+    up_acc[...] = jnp.zeros_like(up_acc)
+    for j in range(4):
+        for d in range(4):
+            if (j, d) != (0, 0):
+                landed(route_all.at[at(source[d] * span + ctx_of[j] * rows, rows)], 6 + 4 * j + d - 1, j, d)
+    lane = lax.broadcasted_iota(jnp.int32, route_all.shape, 1)
+    mine[...] = jnp.sum(jnp.where(lane == c, route_all[...], 0.0), axis=1, keepdims=True)
+
+    def expand(j):
+        block = ctx_of[j]
+
+        def scale(i, _):
+            column = lax.rem(i, tiles)
+            place = at((i // tiles) * span, span)
+            value = hidden[block, place, cols_at(column * tile)].astype(F32)
+            square_sum[place, :] += jnp.sum(value * value, axis=1, keepdims=True)
+            g = gain[:, cols_at(block * cols + column * tile)]
+            scaled[place, cols_at(column * tile)] = (value * g).astype(BF16)
+            return 0
+
+        lax.fori_loop(0, 4 * tiles, scale, 0)
+
+        def step(t, _):
+            unit = cols_at(t * tile)
+            place = at(block * cols, cols)
+            gate_acc[:, unit] += jnp.dot(scaled[...], gate_v[place, unit], preferred_element_type=F32)
+            up_acc[:, unit] += jnp.dot(scaled[...], up_v[place, unit], preferred_element_type=F32)
+            return 0
+
+        lax.fori_loop(0, hidden_units // tile, step, 0)
+
+    for d in (1, 3, 2):
+        landed(block_of(0, d), 33 + d - 1, 0, d)
+        push(block_of(0, d), block_of(0, d), 36 + d, ACROSS)
+        push(block_of(0, d), block_of(0, d), 40 + d, SIB)
+    landed(block_of(ACROSS, 0), 36, ACROSS)
+    push(block_of(ACROSS, 0), block_of(ACROSS, 0), 44, SIB)
+    own_copies[3].wait()
+    own_copies[4].wait()
+    expand(0)
+    for d in (1, 3):
+        landed(block_of(ACROSS, d), 36 + d, ACROSS)
+        push(block_of(ACROSS, d), block_of(ACROSS, d), 44 + d, SIB)
+    for d in range(4):
+        landed(block_of(SIB, d), 40 + d, SIB)
+    expand(1)
+    landed(block_of(ACROSS, 2), 38, ACROSS)
+    push(block_of(ACROSS, 2), block_of(ACROSS, 2), 46, SIB)
+    expand(2)
+    for d in range(4):
+        landed(block_of(DIAG, d), 44 + d, SIB)
+    expand(3)
+
+    def activate(i, _):
+        place = at(i * rows, rows)
+        r = lax.rsqrt(square_sum[place, :] * (1.0 / (4 * cols)) + 1e-06)
+        g = gate_acc[place, :] * r
+        act[place, :] = (g / (1.0 + jnp.exp(-g)) * (up_acc[place, :] * r)).astype(BF16)
+        return 0
+
+    lax.fori_loop(0, 16, activate, 0)
+    own_copies[5].wait()
+
+    def chunk(s, block):
+        return (4 * s + block) * span
+
+    def down(s):
+        target = to[(s + 1) % 4]
+
+        def step(i, _):
+            block, t = i // tiles, lax.rem(i, tiles)
+            y = jnp.dot(
+                act[at(target * span, span), :], down_v[:, cols_at(block * cols + t * tile)],
+                preferred_element_type=F32,
+            )
+            y = y * mine[at(target * span, span), :]
+            work[at(chunk(s, block), span), cols_at(t * tile)] = y.astype(BF16)
+            return 0
+
+        lax.fori_loop(0, 4 * tiles, step, 0)
+        push(work.at[pl.ds(pl.multiple_of(chunk(s, 2 * (1 - k)), span), 2 * span)],
+             core_in.at[s], 48 + s, SIB)
+
+    half = 2 * rows
+
+    def over_x(s):
+        landed(core_in.at[s], 48 + s, SIB)
+
+        def step(i, _):
+            j, t = i // tiles, lax.rem(i, tiles)
+            place, column = at(chunk(s, 2 * k + j), span), cols_at(t * tile)
+            y = work[place, column].astype(F32) + core_in[s, at(j * span, span), column].astype(F32)
+            work[place, column] = y.astype(BF16)
+            return 0
+
+        lax.fori_loop(0, 2 * tiles, step, 0)
+        for j in range(2):
+            push(work.at[at(chunk(s, 2 * k + j) + (1 - x) * half, half)], core_x_in.at[s, j], 52 + 2 * s + j, ACROSS)
+
+    def over_head(s):
+        for j in range(2):
+            landed(core_x_in.at[s, j], 52 + 2 * s + j, ACROSS)
+
+        def step(i, _):
+            j, t = i // tiles, lax.rem(i, tiles)
+            place, column = at(chunk(s, 2 * k + j) + x * half, half), cols_at(t * tile)
+            y = work[place, column].astype(F32) + core_x_in[s, j, :, column].astype(F32)
+            work[place, column] = y.astype(BF16)
+            return 0
+
+        lax.fori_loop(0, 2 * tiles, step, 0)
+        if s < 3:
+            for j in range(2):
+                push(work.at[at(chunk(s, 2 * k + j) + x * half, half)], head_in.at[s, j], 60 + 2 * s + j, 0, s + 1)
+
+    for s in range(4):
+        down(s)
+        if s:
+            over_x(s - 1)
+    over_x(3)
+    for s in range(4):
+        over_head(s)
+    for s in range(3):
+        for j in range(2):
+            landed(head_in.at[s, j], 60 + 2 * s + j, 0, s + 1)
+
+    def total(core, i):
+        j, t = i // tiles, lax.rem(i, tiles)
+        column = cols_at(t * tile)
+        y = work[at(chunk(3, 2 * k + j) + x * half + core * rows, rows), column].astype(F32)
+        for s in range(3):
+            y = y + head_in[s, j, at(core * rows, rows), column].astype(F32)
+        return y
+
+    def other(i, _):
+        last_out[i // tiles, :, cols_at(lax.rem(i, tiles) * tile)] = total(1 - k, i).astype(BF16)
+        return 0
+
+    lax.fori_loop(0, 2 * tiles, other, 0)
+    push(last_out, last_in, 66, SIB)
+
+    def finish(block, i, y):
+        t = lax.rem(i, tiles)
+        kept = hidden[block, at(h * span + c * rows, rows), cols_at(t * tile)].astype(F32)
+        out[:, cols_at(block * cols + t * tile)] = (kept + y).astype(BF16)
+
+    def own(i, _):
+        finish(2 * k + i // tiles, i, total(k, i))
+        return 0
+
+    lax.fori_loop(0, 2 * tiles, own, 0)
+    landed(last_in, 66, SIB)
+
+    def theirs(i, _):
+        y = last_in[i // tiles, :, cols_at(lax.rem(i, tiles) * tile)].astype(F32)
+        finish(2 * (1 - k) + i // tiles, i, y)
+        return 0
+
+    lax.fori_loop(0, 2 * tiles, theirs, 0)
+    for copy in started:
+        copy.wait_send()
+
+
+def local_kernel(attn_out, out_weight, residual, norm_gain, expert_ids, gate_codes, w_gate, w_up, w_down):
+    rows, width = residual.shape
+    depth, cols = out_weight.shape
+    units = w_gate.shape[2]
+    gate_values = gate_codes.astype(F32)
+    route_weights = 2.5 * gate_values / jnp.sum(gate_values, axis=1, keepdims=True)
+    named = expert_ids[:, :, None] == jnp.arange(128, dtype=jnp.int32)
+    weights = jnp.sum(jnp.where(named, route_weights[:, :, None], 0.0), axis=1)
+    span, group = 4 * rows, 16 * rows
+    vmem, hbm = pl.BlockSpec(memory_space=pltpu.VMEM), pl.BlockSpec(memory_space=pl.ANY)
+    return pl.pallas_call(
+        layer_kernel,
+        out_shape=jax.ShapeDtypeStruct((rows, width), BF16),
+        in_specs=[hbm, hbm, hbm, vmem, vmem, hbm, hbm, hbm],
+        out_specs=vmem,
+        scratch_shapes=[
+            pltpu.VMEM((4, span, depth), BF16),
+            pltpu.VMEM((max(depth, 16 * span), cols), BF16),
+            pltpu.VMEM((width, units), BF16),
+            pltpu.VMEM((width, units), BF16),
+            pltpu.VMEM((units, width), BF16),
+            pltpu.VMEM((span, cols), BF16),
+            pltpu.VMEM((4, span, cols), BF16),
+            pltpu.VMEM((3, span, cols), BF16),
+            pltpu.VMEM((4, group, cols), BF16),
+            pltpu.VMEM((group, cols), BF16),
+            pltpu.VMEM((group, units), F32),
+            pltpu.VMEM((group, units), F32),
+            pltpu.VMEM((group, 1), F32),
+            pltpu.VMEM((group, units), BF16),
+            pltpu.VMEM((group, 128), F32),
+            pltpu.VMEM((group, 1), F32),
+            pltpu.VMEM((4, 2 * span, cols), BF16),
+            pltpu.VMEM((4, 2, 2 * rows, cols), BF16),
+            pltpu.VMEM((3, 2, 2 * rows, cols), BF16),
+            pltpu.VMEM((2, rows, cols), BF16),
+            pltpu.VMEM((2, rows, cols), BF16),
+            pltpu.SemaphoreType.DMA((SEMS,)),
+            pltpu.SemaphoreType.DMA((SEMS,)),
+            pltpu.SemaphoreType.DMA((6,)),
+        ],
+        compiler_params=pltpu.CompilerParams(
+            collective_id=0, has_side_effects=True, vmem_limit_bytes=64 * 1024 * 1024,
+        ),
+    )(attn_out, out_weight, residual, norm_gain.reshape(1, width), weights, w_gate, w_up, w_down)
+
+
 def solution(mesh):
     in_specs = (
         P(("groups", "ctx"), "head"),
@@ -84,4 +428,6 @@
         P("ctx", "head", None),
     )
     out_specs = P(("groups", "ctx", "head"), None)
-    return jax.shard_map(local, mesh=mesh, in_specs=in_specs, out_specs=out_specs, check_vma=False)
+    whole_in_vmem = mesh.shape["ctx"] == 4 and mesh.shape["head"] == 4
+    body = local_kernel if whole_in_vmem else local
+    return jax.shard_map(body, mesh=mesh, in_specs=in_specs, out_specs=out_specs, check_vma=False)

time: 617 us -> 202 us (0.33)
  waiting for transfers between devices: 531 us -> 0 us
  Pallas kernels: 0 us -> 196 us
  matrix products: 36.7 us -> 0 us
  blocking collectives: 20.1 us -> 0 us
  between operations: 13.3 us -> 0.01 us
    all_gather x2 -> x0, waiting for transfers between devices: 281 us -> none  [the longest x1 180 us: local(): lax.all_gather(out_weight, 'ctx', axis=1, tiled=True)]
    unnamed x5 -> x0, waiting for transfers between devices: 196 us -> none
    pallas_call x0 -> x1, Pallas kernels: none -> 196 us  [local_kernel(): pl.pallas_call(layer_kernel, out_shape=jax.ShapeDtypeStruct((rows, width)...]
    reduce_scatter x1 -> x0, waiting for transfers between devices: 37.3 us -> none  [local(): lax.psum_scatter(partial_sums.astype(jnp.bfloat16), 'head', scatter_dimen...]
    dot_general x6 -> x0, matrix products: 36.7 us -> none  [the longest x1 14.6 us: local(): jnp.dot(attn_out, lax.all_gather(out_weight, 'ctx', axis=1, tiled=True),...]
    all_to_all x1 -> x0, blocking collectives: 20.1 us -> none  [local(): lax.all_to_all(outbound, 'ctx', split_axis=0, concat_axis=0, tiled=True)]
    all_to_all x1 -> x0, waiting for transfers between devices: 15.9 us -> none  [local(): lax.all_to_all(summed_out.reshape(ctx_count, capacity, model_width).astyp...]
  transfers between devices with their start and end apart: 5 -> 0, of which waited for: 5 -> 0; matrix products, arithmetic and copies ran while one was open for 0% -> 0% of each run, Pallas kernels for 0% -> 0%
where the time goes in v2:
time: 202 us; the launch traced here: 201 us
  Pallas kernels  196 us (97%)
  other arithmetic  2.75 us (1%)
    pallas_call x1, Pallas kernels, local_kernel(): pl.pallas_call(layer_kernel, out_shape=jax.ShapeDtypeStruct((rows, width)...  196 us

profile of v2, /device:TPU:27, one launch (start us, length us, event | category | flops | bytes accessed | tf_op | source)
XLA Modules:
  0.0 200.6 jit_solution(8862812094118129223)
XLA Ops:
  0.0 0.7 convert_reduce_fusion
  0.7 0.7 multiply_divide_fusion
  1.4 1.4 select_reduce_fusion.route_w
  2.8 196.0 %shard_map.91 = bf16[32,7168]{1,0:T(8,128)(2,1)} custom-call(bf16[128,2048]{1,0:T(8,128)(2,1)} %attn.1, bf16[2048,1792]{1,0:T(8,128)(2,1)} %out_w.1, bf16[32,7168]{1,0:T(8,128)(2,1)} %resid.1, f32[1,7168]{1,0:T(1,128)} %bitcast.1, f32[32,128]{1,0:T(8,128)} %select_reduce_fusion.route_w, bf16[1,7168,512]{2,1,0:T(8,128)(2,1)} %gate_w.1, ...), custom_call_target="tpu_custom_call" | custom-call | tf_op jit(solution)/shard_map/pallas_call | solution.py:381
  198.8 1.8 copy.13

commit v3 on v2

--- a/solution.py
+++ b/solution.py
@@ -138,7 +138,7 @@
         pltpu.make_async_copy(up_w.at[0], up_v, local_sem.at[4]),
         pltpu.make_async_copy(down_w.at[0], down_v, local_sem.at[5]),
     ]
-    for copy in own_copies:
+    for copy in own_copies[:3]:
         copy.start()
     pl.semaphore_wait(barrier, 15)
 
@@ -169,6 +169,8 @@
 
     own_copies[0].wait()
     own_copies[1].wait()
+    for copy in own_copies[3:]:
+        copy.start()
     project(0)
     landed(attn_all.at[ctx_of[SIB]], 1, SIB)
     project(1)
@@ -195,13 +197,25 @@
 
     lax.fori_loop(0, tiles, add_up, 0)
 
-    def block_of(j, d):
-        return hidden.at[ctx_of[j], at(source[d] * span, span)]
-
-    for d in (2, 1, 3):
-        push(block_of(0, 0), block_of(0, 0), 33 + d - 1, 0, d)
-    push(block_of(0, 0), block_of(0, 0), 36, ACROSS)
-    push(block_of(0, 0), block_of(0, 0), 40, SIB)
+    def block_of(j, b):
+        return hidden.at[ctx_of[j], at(b * span, span)]
+
+    def line(b, number, step):
+        return pltpu.make_async_remote_copy(
+            src_ref=block_of(0, b), dst_ref=block_of(0, b), send_sem=send.at[number], recv_sem=recv.at[number],
+            device_id={"ctx": c, "head": h + step}, device_id_type=pl.DeviceIdType.MESH,
+        )
+
+    def pass_on(b):
+        remote(block_of(0, b), block_of(0, b), 36 + b, ACROSS).start()
+        remote(block_of(0, b), block_of(0, b), 40 + b, SIB).start()
+
+    def streams(i):
+        return ((h - i, h - i >= 0, h < 3, 33, 1), (h + i, h + i <= 3, h > 0, 67, -1))
+
+    for b, there, onward, first, step in streams(0):
+        pl.when(onward)(lambda b=b, first=first, step=step: line(b, first, step).start())
+    pass_on(h)
 
     square_sum[...] = jnp.zeros_like(square_sum)
     gate_acc[...] = jnp.zeros_like(gate_acc)
@@ -236,26 +250,38 @@
 
         lax.fori_loop(0, hidden_units // tile, step, 0)
 
-    for d in (1, 3, 2):
-        landed(block_of(0, d), 33 + d - 1, 0, d)
-        push(block_of(0, d), block_of(0, d), 36 + d, ACROSS)
-        push(block_of(0, d), block_of(0, d), 40 + d, SIB)
-    landed(block_of(ACROSS, 0), 36, ACROSS)
-    push(block_of(ACROSS, 0), block_of(ACROSS, 0), 44, SIB)
+    for i in (1, 2, 3):
+        for b, there, onward, first, step in streams(i):
+
+            @pl.when(there)
+            def _():
+                line(b, first + i - 1, -step).wait_recv()
+                if i < 3:
+                    pl.when(onward)(lambda: line(b, first + i, step).start())
+                pass_on(b)
+
+    def to_sibling(i):
+        for b, there, onward, first, step in streams(i):
+
+            @pl.when(there)
+            def _():
+                remote(block_of(ACROSS, b), block_of(ACROSS, b), 36 + b, ACROSS).wait_recv()
+                remote(block_of(ACROSS, b), block_of(ACROSS, b), 44 + b, SIB).start()
+
+    remote(block_of(ACROSS, h), block_of(ACROSS, h), 36 + h, ACROSS).wait_recv()
+    remote(block_of(ACROSS, h), block_of(ACROSS, h), 44 + h, SIB).start()
+    to_sibling(1)
     own_copies[3].wait()
     own_copies[4].wait()
     expand(0)
-    for d in (1, 3):
-        landed(block_of(ACROSS, d), 36 + d, ACROSS)
-        push(block_of(ACROSS, d), block_of(ACROSS, d), 44 + d, SIB)
-    for d in range(4):
-        landed(block_of(SIB, d), 40 + d, SIB)
+    for b in range(4):
+        landed(block_of(SIB, b), 40 + b, SIB)
+    to_sibling(2)
     expand(1)
-    landed(block_of(ACROSS, 2), 38, ACROSS)
-    push(block_of(ACROSS, 2), block_of(ACROSS, 2), 46, SIB)
+    to_sibling(3)
     expand(2)
-    for d in range(4):
-        landed(block_of(DIAG, d), 44 + d, SIB)
+    for b in range(4):
+        landed(block_of(DIAG, b), 44 + b, SIB)
     expand(3)
 
     def activate(i, _):
@@ -274,19 +300,22 @@
     def down(s):
         target = to[(s + 1) % 4]
 
-        def step(i, _):
-            block, t = i // tiles, lax.rem(i, tiles)
-            y = jnp.dot(
-                act[at(target * span, span), :], down_v[:, cols_at(block * cols + t * tile)],
-                preferred_element_type=F32,
-            )
-            y = y * mine[at(target * span, span), :]
-            work[at(chunk(s, block), span), cols_at(t * tile)] = y.astype(BF16)
-            return 0
-
-        lax.fori_loop(0, 4 * tiles, step, 0)
-        push(work.at[pl.ds(pl.multiple_of(chunk(s, 2 * (1 - k)), span), 2 * span)],
-             core_in.at[s], 48 + s, SIB)
+        def half_of(core):
+            def step(i, _):
+                block, t = 2 * core + i // tiles, lax.rem(i, tiles)
+                y = jnp.dot(
+                    act[at(target * span, span), :], down_v[:, cols_at(block * cols + t * tile)],
+                    preferred_element_type=F32,
+                )
+                y = y * mine[at(target * span, span), :]
+                work[at(chunk(s, block), span), cols_at(t * tile)] = y.astype(BF16)
+                return 0
+
+            lax.fori_loop(0, 2 * tiles, step, 0)
+
+        half_of(1 - k)
+        push(work.at[pl.ds(pl.multiple_of(chunk(s, 2 * (1 - k)), span), 2 * span)], core_in.at[s], 48 + s, SIB)
+        half_of(k)
 
     half = 2 * rows
 
@@ -322,9 +351,7 @@
 
     for s in range(4):
         down(s)
-        if s:
-            over_x(s - 1)
-    over_x(3)
+        over_x(s)
     for s in range(4):
         over_head(s)
     for s in range(3):
@@ -366,6 +393,13 @@
     lax.fori_loop(0, 2 * tiles, theirs, 0)
     for copy in started:
         copy.wait_send()
+    for b in range(4):
+        remote(block_of(0, b), block_of(0, b), 36 + b, ACROSS).wait_send()
+        remote(block_of(0, b), block_of(0, b), 40 + b, SIB).wait_send()
+        remote(block_of(ACROSS, b), block_of(ACROSS, b), 44 + b, SIB).wait_send()
+    for i in range(3):
+        for b, there, onward, first, step in streams(i):
+            pl.when(there & onward)(lambda: line(b, first + i, step).wait_send())
 
 
 def local_kernel(attn_out, out_weight, residual, norm_gain, expert_ids, gate_codes, w_gate, w_up, w_down):

time: 202 us -> 184 us (0.911)
  Pallas kernels: 196 us -> 180 us
    pallas_call x1, Pallas kernels: 196 us -> 180 us  [local_kernel(): pl.pallas_call(layer_kernel, out_shape=jax.ShapeDtypeStruct((rows, width)...]
where the time goes in v3:
time: 184 us
  Pallas kernels  180 us (98%)
  other arithmetic  2.75 us (1%)
    pallas_call x1, Pallas kernels, local_kernel(): pl.pallas_call(layer_kernel, out_shape=jax.ShapeDtypeStruct((rows, width)...  180 us

profile of v3, /device:TPU:27, one launch (start us, length us, event | category | flops | bytes accessed | tf_op | source)
XLA Modules:
  0.0 184.1 jit_solution(493611831896992601)
XLA Ops:
  0.0 0.7 convert_reduce_fusion
  0.7 0.7 multiply_divide_fusion
  1.4 1.4 select_reduce_fusion.route_w
  2.8 179.5 %shard_map.91 = bf16[32,7168]{1,0:T(8,128)(2,1)} custom-call(bf16[128,2048]{1,0:T(8,128)(2,1)} %attn.1, bf16[2048,1792]{1,0:T(8,128)(2,1)} %out_w.1, bf16[32,7168]{1,0:T(8,128)(2,1)} %resid.1, f32[1,7168]{1,0:T(1,128)} %bitcast.1, f32[32,128]{1,0:T(8,128)} %select_reduce_fusion.route_w, bf16[1,7168,512]{2,1,0:T(8,128)(2,1)} %gate_w.1, ...), custom_call_target="tpu_custom_call" | custom-call | tf_op jit(solution)/shard_map/pallas_call | solution.py:415
  182.3 1.8 copy.13

commit v4 on v3

--- a/solution.py
+++ b/solution.py
@@ -351,7 +351,9 @@
 
     for s in range(4):
         down(s)
-        over_x(s)
+        if s:
+            over_x(s - 1)
+    over_x(3)
     for s in range(4):
         over_head(s)
     for s in range(3):

time: 184 us -> 184 us (level)
  no operation moved by 1% of the time
where the time goes in v4:
time: 184 us
  Pallas kernels  179 us (97%)
  other arithmetic  2.75 us (1%)
    pallas_call x1, Pallas kernels, local_kernel(): pl.pallas_call(layer_kernel, out_shape=jax.ShapeDtypeStruct((rows, width)...  179 us

profile of v4, /device:TPU:27, one launch (start us, length us, event | category | flops | bytes accessed | tf_op | source)
XLA Modules:
  0.0 184.0 jit_solution(7629005953515946850)
XLA Ops:
  0.0 0.7 convert_reduce_fusion
  0.7 0.7 multiply_divide_fusion
  1.4 1.4 select_reduce_fusion.route_w
  2.8 179.4 %shard_map.91 = bf16[32,7168]{1,0:T(8,128)(2,1)} custom-call(bf16[128,2048]{1,0:T(8,128)(2,1)} %attn.1, bf16[2048,1792]{1,0:T(8,128)(2,1)} %out_w.1, bf16[32,7168]{1,0:T(8,128)(2,1)} %resid.1, f32[1,7168]{1,0:T(1,128)} %bitcast.1, f32[32,128]{1,0:T(8,128)} %select_reduce_fusion.route_w, bf16[1,7168,512]{2,1,0:T(8,128)(2,1)} %gate_w.1, ...), custom_call_target="tpu_custom_call" | custom-call | tf_op jit(solution)/shard_map/pallas_call | solution.py:417
  182.2 1.8 copy.13
